TPU v7x, 512 devices: a whole 4x8x8 slice. The times are simulated.
512 devices in a mesh: src: 32 (over y, x), tgt: 16 (over z, core).
Axes of the slice: x: 4, y: 8, z: 8, core: 2. Of those that a mesh axis runs over, the one named last changes fastest.
Arguments:
- features: bfloat16 [65536, 128], P(('tgt', 'src')), may hold values from -8 to 8
- adjacency: bfloat16 [16, 32, 128, 128, 128], P('tgt', 'src'), may hold values from 0 to 600, as said below
- tile_slot: int32 [16, 32, 128], P('tgt', 'src'), may hold values from 0 to 511, as said below
- tile_live: int32 [16, 32, 128], P('tgt', 'src'), may hold values from 0 to 1, as said below
- first_weight: bfloat16 [128, 256], replicated, may hold values from -0.5 to 0.5
- second_weight: bfloat16 [256, 256], replicated, may hold values from -0.375 to 0.375
Outputs:
- embedding: bfloat16 [65536, 256], P(('tgt', 'src'))
Inputs may be any that keep to these rules, and one draw needn't show every extreme that they name: `adjacency`: nonnegative edge weights; on average about min(0.3, 4 / 128) of a tile's entries are nonzero. `tile_slot`: a slot's value is local target block * 16 + local source block. `tile_live`: on each device the live slots come first; each device has 32 to 128 live slots, and some device has all 128 live.
All inputs are finite; a program needn't handle non-finite values.
Results may differ from a plain program's by a relative error of at most 0.023.
Values may be sent and summed in bfloat16 or wider, within the bound.
A program may use at most 64 MiB of HBM per device.

v0:
```python
import jax
import jax.numpy as jnp
from jax import lax
from jax.sharding import PartitionSpec as P

tile_group = 8


def spread(gathered, adjacency, slot_index, slot_live, target_blocks):
    tile_edge = adjacency.shape[-1]
    feature_width = gathered.shape[1]
    source_blocks = gathered.reshape(-1, tile_edge, feature_width)
    source_count = source_blocks.shape[0]

    def one_group(number, accumulated):
        offset = number * tile_group
        part_tiles = lax.dynamic_slice_in_dim(adjacency, offset, tile_group, 0)
        part_slots = lax.dynamic_slice_in_dim(slot_index, offset, tile_group, 0)
        part_live = lax.dynamic_slice_in_dim(slot_live, offset, tile_group, 0).astype(jnp.float32)
        sources = source_blocks[part_slots % source_count]
        products = jnp.einsum(
            "tij,tjf->tif", part_tiles, sources, preferred_element_type=jnp.float32
        )
        products = products * part_live[:, None, None]
        return accumulated.at[part_slots // source_count].add(products)

    starting = jnp.zeros((target_blocks, tile_edge, feature_width), jnp.float32)
    trip_count = adjacency.shape[0] // tile_group
    result = lax.fori_loop(0, trip_count, one_group, starting)
    return result.reshape(target_blocks * tile_edge, feature_width)


def convolve(hidden, weight, inverse_root, adjacency, slot_index, slot_live, target_blocks):
    scaled = (inverse_root[:, None] * hidden.astype(jnp.float32)).astype(jnp.bfloat16)
    gathered = lax.all_gather(scaled, "tgt", axis=0, tiled=True)
    partial_value = spread(gathered, adjacency, slot_index, slot_live, target_blocks)
    summed = lax.psum_scatter(
        partial_value.astype(jnp.bfloat16), "src", scatter_dimension=0, tiled=True
    ).astype(jnp.float32)
    combined = (inverse_root[:, None] * (summed + scaled.astype(jnp.float32))).astype(jnp.bfloat16)
    return jax.nn.relu(jnp.dot(combined, weight, preferred_element_type=jnp.float32)).astype(
        jnp.bfloat16
    )


def on_device(features, adjacency, tile_slot, tile_live, first_weight, second_weight):
    own_tiles = adjacency[0, 0]
    slot_index = tile_slot[0, 0]
    slot_live = tile_live[0, 0]
    own_rows = features.shape[0]
    tile_edge = own_tiles.shape[-1]
    target_blocks = own_rows * lax.axis_size("src") // tile_edge
    source_count = own_rows * lax.axis_size("tgt") // tile_edge
    row_totals = jnp.sum(own_tiles, axis=2, dtype=jnp.float32) * slot_live[:, None].astype(
        jnp.float32
    )
    local_degree = (
        jnp.zeros((target_blocks, tile_edge), jnp.float32)
        .at[slot_index // source_count]
        .add(row_totals)
    )
    local_degree = local_degree.reshape(-1)
    degree = lax.psum_scatter(local_degree, "src", scatter_dimension=0, tiled=True)
    inverse_root = lax.rsqrt(1.0 + degree)
    hidden = convolve(
        features, first_weight, inverse_root, own_tiles, slot_index, slot_live, target_blocks
    )
    return convolve(
        hidden, second_weight, inverse_root, own_tiles, slot_index, slot_live, target_blocks
    )


def solution(mesh):
    placed = (
        P(("tgt", "src"), None),
        P("tgt", "src", None, None, None),
        P("tgt", "src", None),
        P("tgt", "src", None),
        P(),
        P(),
    )
    return jax.shard_map(
        on_device, mesh=mesh, in_specs=placed, out_specs=P(("tgt", "src"), None), check_vma=False
    )
```

profile of v0, /device:TPU:16, one launch (start us, length us, event | category | flops | bytes accessed | tf_op | source)
XLA Modules:
  0.0 806.3 jit_solution(8807981930895791408)
XLA Ops:
  7.9 3.4 convert_reduce_fusion
  12.4 131.0 %all-reduce = f32[4096]{0:T(1024)S(1)} all-reduce(f32[4096]{0:T(1024)S(1)} %bitcast.37), channel_id=2, replica_groups=mesh['src'=32,'tgt'=16] {'src'}, use_global_device_ids=true, to_apply=%region_2.3.clone | all-reduce | flops 4096 | bytes 32768
  143.4 1.3 dynamic-slice
  146.0 24.6 %all_gather.6 = bf16[2048,128]{1,0:T(8,128)(2,1)S(1)} all-gather(bf16[128,128]{1,0:T(8,128)(2,1)S(1)} %multiply_convert_fusion.3), channel_id=1, replica_groups=mesh['src'=32,'tgt'=16] {'tgt'}, dimensions={0}, use_global_device_ids=true | all-gather | bytes 557056 | tf_op jit(solution)/shard_map/all_gather | solution.py:35
  170.9 48.4 %while.30 = (s32[]{:T(128)}, f32[32,128,128]{2,1,0:T(8,128)S(1)}, s32[128]{0:T(128)S(1)}, bf16[128,128,128]{2,1,0:T(8,128)(2,1)}, bf16[16,128,128]{2,1,0:T(8,128...) while((s32[]{:T(128)}, f32[32,128,128]{2,1,0:T(8,128)S(1)}, ...), condition=%wide.region_5.6_spmd, body=%wide.region_3.5_spmd.sunk | while | flops 33817844 | bytes 3150367 | solution.py:29
  174.7 1.2 convolution_multiply_fusion.4
  183.8 1.2 convolution_multiply_fusion.4
  186.8 1.2 convolution_multiply_fusion.4
  220.5 223.2 %reduce-scatter.3.cloned.1.call-done = bf16[128,128]{1,0:T(8,128)(2,1)} async-done(((bf16[4096,128]{1,0:T(8,128)(2,1)}), bf16[128,128]{1,0:T(8,128)(2,1)}) %reduce-scatter.3.cloned.1.call-update) | async-done | bytes 32784 | tf_op jit(solution)/shard_map/reduce_scatter | solution.py:37
  443.7 1.6 fusion.7
  445.4 41.2 %all-gather.2.cloned.1.call-done = bf16[2048,256]{1,0:T(8,128)(2,1)} async-done(((bf16[128,256]{1,0:T(8,128)(2,1)}), bf16[2048,256]{1,0:T(8,128)(2,1)}) %all-gather.2.cloned.1.call-update) | async-done | bytes 1048592 | tf_op jit(solution)/shard_map/all_gather | solution.py:35
  486.6 2.4 broadcast_in_dim.61
  489.1 85.3 %while.31 = (s32[]{:T(128)}, f32[32,128,256]{2,1,0:T(8,128)}, s32[128]{0:T(128)S(1)}, bf16[128,128,128]{2,1,0:T(8,128)(2,1)}, bf16[16,128,256]{2,1,0:T(8,128)(2,...) while((s32[]{:T(128)}, f32[32,128,256]{2,1,0:T(8,128)}, s32[128]{0:T(128)S(1)}, ...), condition=%wide.region_9.10_spmd, body=%wide.region_7.9_spmd.sunk | while | flops 67634424 | bytes 6033951 | solution.py:29
  489.8 1.2 convolution_multiply_fusion.5
  491.1 3.3 scatter_fusion.1
  495.2 1.2 convolution_multiply_fusion.5
  496.4 3.4 scatter_fusion.1
  500.5 1.2 convolution_multiply_fusion.5
  501.8 3.3 scatter_fusion.1
  505.9 1.2 convolution_multiply_fusion.5
  507.1 3.3 scatter_fusion.1
  511.2 1.2 convolution_multiply_fusion.5
  512.5 3.4 scatter_fusion.1
  516.6 1.2 convolution_multiply_fusion.5
  517.9 3.4 scatter_fusion.1
  522.0 1.2 convolution_multiply_fusion.5
  523.2 3.3 scatter_fusion.1
  527.3 1.2 convolution_multiply_fusion.5
  528.5 3.3 scatter_fusion.1
  532.6 1.2 convolution_multiply_fusion.5
  533.9 3.3 scatter_fusion.1
  538.0 1.2 convolution_multiply_fusion.5
  539.2 3.3 scatter_fusion.1
  543.3 1.2 convolution_multiply_fusion.5
  544.6 3.3 scatter_fusion.1
  548.7 1.2 convolution_multiply_fusion.5
  549.9 3.3 scatter_fusion.1
  554.0 1.2 convolution_multiply_fusion.5
  555.2 3.2 scatter_fusion.1
  559.2 1.2 convolution_multiply_fusion.5
  560.5 3.3 scatter_fusion.1
  564.5 1.2 convolution_multiply_fusion.5
  565.8 3.3 scatter_fusion.1
  569.8 1.2 convolution_multiply_fusion.5
  571.1 3.3 scatter_fusion.1
  574.3 3.8 convert_element_type.91
  578.2 219.9 %reduce-scatter.5.cloned.1.call-done = bf16[128,256]{1,0:T(8,128)(2,1)} async-done(((bf16[4096,256]{1,0:T(8,128)(2,1)}), bf16[128,256]{1,0:T(8,128)(2,1)}) %reduce-scatter.5.cloned.1.call-update) | async-done | bytes 65552 | tf_op jit(solution)/shard_map/reduce_scatter | solution.py:37
  798.1 1.7 fusion.8
  (190 shorter events, 60.8 us)
Async XLA Ops:
  6.5 791.6 %copy-start = (bf16[256,256]{1,0:T(8,128)(2,1)S(1)}, bf16[256,256]{1,0:T(8,128)(2,1)}, u32[]{:S(2)}) copy-start(bf16[256,256]{1,0:T(8,128)(2,1)} %param.15) | copy-start | bytes 393220
  6.5 164.3 %copy-start.3 = (s32[1,1,128]{2,1,0:T(1,128)S(1)}, s32[1,1,128]{2,1,0:T(1,128)}, u32[]{:S(2)}) copy-start(s32[1,1,128]{2,1,0:T(1,128)} %param.12) | copy-start | bytes 1540
  6.5 164.3 %copy-start.4 = (s32[1,1,128]{2,1,0:T(1,128)S(1)}, s32[1,1,128]{2,1,0:T(1,128)}, u32[]{:S(2)}) copy-start(s32[1,1,128]{2,1,0:T(1,128)} %param.13) | copy-start | bytes 1540
  6.5 139.4 %copy-start.5 = (bf16[128,128]{1,0:T(8,128)(2,1)S(1)}, bf16[128,128]{1,0:T(8,128)(2,1)}, u32[]{:S(2)}) copy-start(bf16[128,128]{1,0:T(8,128)(2,1)} %param.10) | copy-start | bytes 98308
  6.5 437.2 %reduce-scatter.3.cloned.1.call-start = ((), (), s32[]{:S(2)}) async-start(), calls=%async_computation.2 | async-start | bytes 1081344 | tf_op jit(solution)/shard_map/reduce_scatter | solution.py:37
  145.4 0.5 copy-start.7
  219.3 224.5 %copy-start.6 = (bf16[128,128]{1,0:T(8,128)(2,1)S(1)}, bf16[128,128]{1,0:T(8,128)(2,1)}, u32[]{:S(2)}) copy-start(bf16[128,128]{1,0:T(8,128)(2,1)} %param.10) | copy-start | bytes 98308
  219.3 224.5 %copy-start.8 = (f32[128]{0:T(128)S(1)}, f32[128]{0:T(128)}, u32[]{:S(2)}) copy-start(f32[128]{0:T(128)} %copy-done.7) | copy-start | bytes 1540
  219.3 224.4 %copy-start.9 = (bf16[128,256]{1,0:T(8,128)(2,1)S(1)}, bf16[128,256]{1,0:T(8,128)(2,1)}, u32[]{:S(2)}) copy-start(bf16[128,256]{1,0:T(8,128)(2,1)} %param.14) | copy-start | bytes 196612
  220.5 266.2 %all-gather.2.cloned.1.call-start = ((), (), s32[]{:S(2)}) async-start(), calls=%async_computation.3 | async-start | bytes 1114112 | tf_op jit(solution)/shard_map/all_gather | solution.py:35
  445.4 352.7 %reduce-scatter.5.cloned.1.call-start = ((), (), s32[]{:S(2)}) async-start(), calls=%async_computation.4 | async-start | bytes 2162688 | tf_op jit(solution)/shard_map/reduce_scatter | solution.py:37
  486.6 2.4 copy-start.1
  574.3 223.8 %copy-start.2 = (bf16[128,256]{1,0:T(8,128)(2,1)S(1)}, bf16[128,256]{1,0:T(8,128)(2,1)}, u32[]{:S(2)}) copy-start(bf16[128,256]{1,0:T(8,128)(2,1)} %fusion.7) | copy-start | bytes 196612
Sparse Core Ops, SparseCore 0:
  220.6 223.0 reduce-scatter.2
  445.8 40.7 all-gather.1
  578.3 219.7 reduce-scatter.4
where the time goes:
time: 808 us; the launch traced here: 806 us
  waiting for transfers between devices  484 us (60%)
  blocking collectives  156 us (19%)
  other arithmetic  86 us (11%)
  matrix products  42 us (5%)
  local copies, waits for them, and re-layouts  23.3 us (3%)
  between operations  13.9 us (2%)
    reduce_scatter x2, waiting for transfers between devices, convolve(): lax.psum_scatter(partial_value.astype(jnp.bfloat16), 'src', scatter_dimen...  443 us
    unnamed x1, blocking collectives  131 us
    scatter-add x32, other arithmetic, one_group(): return accumulated.at[part_slots // source_count].add(products)  69.6 us
    all_gather x1, waiting for transfers between devices, convolve(): gathered = lax.all_gather(scaled, 'tgt', axis=0, tiled=True)  41.2 us
    dot_general x32, matrix products, one_group(): jnp.einsum('tij,tjf->tif', part_tiles, sources, preferred_element_type=jn...  38.7 us
    all_gather x1, blocking collectives, convolve(): gathered = lax.all_gather(scaled, 'tgt', axis=0, tiled=True)  24.6 us
    gather x32, local copies, waits for them, and re-layouts, one_group(): sources = source_blocks[part_slots % source_count]  18.9 us
  transfers between devices with their start and end apart: 3, of which 3 were waited for; matrix products, arithmetic and copies ran while one was open for 0% of the time, Pallas kernels for 0%

commit v1 on v0

v1 whole, which is shorter than its diff:
```python
import functools

import jax
import jax.numpy as jnp
from jax import lax
from jax.experimental import pallas as pl
from jax.experimental.pallas import tpu as pltpu
from jax.sharding import PartitionSpec as P

MESH = pl.DeviceIdType.MESH
F32 = jnp.float32
BF16 = jnp.bfloat16
NX = 4
B = 128
H = B // 2
LOADS = 4


def wrap(a, n):
    return lax.rem(a + n, n)


def plan(nx, ny, nz, width1, width2):
    ns = 2 * nz
    rows = [
        ("dx_send", (nx, ny, B), F32),
        ("dx_recv", (nx, ny, B), F32),
        ("dy_send", (ny, 8, B), F32),
        ("dy_recv", (ny, 8, B), F32),
        ("roots", (ns, 8, B), F32),
        ("src1", (ns, B, width1), BF16),
        ("src2", (ns, B, width2), BF16),
    ]
    for layer, width in ((1, width1), (2, width2)):
        for chain, (n1, n2) in (("a", (ny, nx)), ("b", (nx, ny))):
            for way, steps in ((0, n1 // 2), (1, (n1 - 1) // 2)):
                for end in ("send", "recv"):
                    rows.append((f"{chain}1{way}{layer}{end}", (max(steps, 1), n2, H, width), BF16))
            for way, steps in ((0, n2 // 2), (1, (n2 - 1) // 2)):
                for end in ("send", "recv"):
                    rows.append((f"{chain}2{way}{layer}{end}", (max(steps, 1), H, width), BF16))
    return rows


class Links:
    def __init__(self, send_sems, recv_sems):
        self.send_sems, self.recv_sems = send_sems, recv_sems
        self.count = 0
        self.sent = []

    def copy(self, src, dst, device):
        number = self.count
        self.count += 1
        made = pltpu.make_async_remote_copy(
            src_ref=src,
            dst_ref=dst,
            send_sem=self.send_sems.at[number],
            recv_sem=self.recv_sems.at[number],
            device_id=device,
            device_id_type=MESH,
        )
        made.start()
        self.sent.append(made)
        return made

    def finish(self):
        for made in self.sent:
            made.wait_send()


def order(slot, live, nb, count):
    lane = lax.broadcasted_iota(jnp.int32, (B, B), 1)
    sub = lax.broadcasted_iota(jnp.int32, (B, B), 0)
    value = jnp.broadcast_to(jnp.where(live > 0, slot, nb), (B, B))
    value_t = value.T
    key, key_t = value * count + lane, value_t * count + sub
    rank = jnp.sum((key_t < key).astype(jnp.int32), axis=0, keepdims=True)
    chosen = (jnp.broadcast_to(rank, (B, B)).T == lane).astype(jnp.int32)
    rows = [
        jnp.sum(chosen * sub, axis=0, keepdims=True),
        jnp.sum(chosen * value_t, axis=0, keepdims=True),
    ]
    for j in range(-(-nb // B)):
        block = lane + j * B
        upto = jnp.sum((value_t <= block).astype(jnp.int32), axis=0, keepdims=True)
        below = jnp.sum((value_t < block).astype(jnp.int32), axis=0, keepdims=True)
        rows.append(jnp.where(upto > below, upto - 1, count))
    while len(rows) < 8:
        rows.append(jnp.zeros((1, B), jnp.int32))
    return value, jnp.concatenate(rows, axis=0)


def kernel(dims, names, feat, adj, slot, live, w1, w2, out, *scratch):
    nx, ny, nz = dims
    nt, ns = nx * ny, 2 * nz
    nb = nt * ns
    count = adj.shape[0]
    buf = dict(zip(names, scratch))
    (tiles, sums, rowsum, dense_a, dense_b, acc_a0, acc_a1, acc_a2, acc_b0, acc_b1, acc_b2,
     ready1, scaled1, index_v, index_s, load_sems, index_sem, send_sems, recv_sems) = scratch[len(names):]
    accs_a, accs_b = (acc_a0, acc_a1, acc_a2), (acc_b0, acc_b1, acc_b2)
    links = Links(send_sems, recv_sems)

    me_s, me_t = lax.axis_index("src"), lax.axis_index("tgt")
    y, x = me_s // nx, lax.rem(me_s, nx)
    z, core = me_t // 2, lax.rem(me_t, 2)
    sign = 1 - 2 * core

    def at_x(d):
        return {"src": y * nx + wrap(x + d, nx)}

    def at_y(d):
        return {"src": wrap(y + d, ny) * nx + x}

    def at_z(d):
        return {"tgt": wrap(z + d, nz) * 2 + core}

    sibling = {"tgt": z * 2 + 1 - core}

    per_load = count // LOADS
    loads = []
    for j in range(LOADS):
        part = pl.ds(j * per_load, per_load)
        loads.append(pltpu.make_async_copy(adj.at[part], tiles.at[part], load_sems.at[j]))
        loads[-1].start()
    barrier = pltpu.get_barrier_semaphore()
    greeted = 0
    for d in range(1, nx):
        pl.semaphore_signal(barrier, inc=1, device_id=at_x(d), device_id_type=MESH)
        greeted += 1
    for d in range(1, ny):
        pl.semaphore_signal(barrier, inc=1, device_id=at_y(d), device_id_type=MESH)
        greeted += 1
    for d in range(1, ns):
        pl.semaphore_signal(
            barrier, inc=1, device_id={"tgt": lax.rem(me_t + d, ns)}, device_id_type=MESH
        )
        greeted += 1

    value, found = order(slot[...], live[...], nb, count)
    index_v[...] = found
    to_smem = pltpu.make_async_copy(index_v, index_s, index_sem)
    to_smem.start()

    buf["src1"][me_t] = feat[...]
    pl.semaphore_wait(barrier, greeted)

    def gather_start(ref, first, size):
        part = pl.ds(first, size)
        state = {"ref": ref, "part": part, "long": [], "short": [], "sibling": []}
        mine = ref.at[me_t, part]
        state["sibling"].append(links.copy(mine, mine, sibling))
        if nz > 1:
            state["long"].append(links.copy(mine, mine, at_z(sign)))
        if (nz - 1) // 2:
            state["short"].append(links.copy(mine, mine, at_z(-sign)))
        return state

    def gather_step(state, k):
        ref = state["ref"]
        for way, steps, d in (("long", nz // 2, sign), ("short", (nz - 1) // 2, -sign)):
            if k < steps:
                state[way][k].wait_recv()
                got = ref.at[wrap(z - d * (k + 1), nz) * 2 + core, state["part"]]
                if k + 1 < steps:
                    state[way].append(links.copy(got, got, at_z(d)))
                state["sibling"].append(links.copy(got, got, sibling))

    def gather_finish(state):
        for made in state["sibling"]:
            made.wait_recv()

    gathered = gather_start(buf["src1"], 0, B)

    ones = jnp.ones((8, B), BF16)
    group = min(16, per_load)
    for j in range(LOADS):
        loads[j].wait()

        def sum_rows(i, carry, j=j):
            first = j * per_load + i * group
            part = tiles[pl.ds(first, group)].reshape(group * B, B)
            got = lax.dot_general(ones, part, (((1,), (1,)), ((), ())), preferred_element_type=F32)
            for q in range(group):
                rowsum[first // group, q : q + 1, :] = got[0:1, q * B : (q + 1) * B]
            return carry

        lax.fori_loop(0, per_load // group, sum_rows, 0)
    row = lax.broadcasted_iota(jnp.int32, (nt, B), 0)
    target = lax.rem(row, ny) * nx + row // ny
    value_row = value[0:1]
    mine = (value_row >= target * ns) & (value_row < (target + 1) * ns)
    degree = jnp.dot(
        mine.astype(F32),
        rowsum[...].reshape(count, B),
        preferred_element_type=F32,
        precision=lax.Precision.HIGHEST,
    )
    for i in range(nx):
        buf["dx_send"][i] = degree[i * ny : (i + 1) * ny]
    dx = [
        links.copy(buf["dx_send"].at[wrap(x + d, nx)], buf["dx_recv"].at[d], at_x(d))
        for d in range(1, nx)
    ]

    to_smem.wait()
    sums[count] = jnp.zeros((B, B), BF16)

    def add_tile(i, carry):
        before, total = carry
        now = index_s[1, i]
        same = jnp.where(now == before, 1.0, 0.0).astype(F32)
        total = tiles[jnp.clip(index_s[0, i], 0, count - 1)].astype(F32) + total * same
        sums[i] = total.astype(BF16)
        return now, total

    lax.fori_loop(0, count, add_tile, (jnp.int32(-1), jnp.zeros((B, B), F32)), unroll=2)

    for made in dx:
        made.wait_recv()
    part = buf["dx_send"][x]
    for d in range(1, nx):
        part = part + buf["dx_recv"][d]
    for i in range(ny):
        buf["dy_send"][i] = jnp.broadcast_to(part[i : i + 1], (8, B))
    dy = [
        links.copy(buf["dy_send"].at[wrap(y + d, ny)], buf["dy_recv"].at[d], at_y(d))
        for d in range(1, ny)
    ]
    gather_step(gathered, 0)

    def place(t, carry):
        ty, tx = t // nx, lax.rem(t, nx)
        for c in range(ns):
            v = t * ns + c
            tile = sums[jnp.clip(index_s[2 + v // B, lax.rem(v, B)], 0, count)]
            dense_a[ty, tx, :, c * B : (c + 1) * B] = tile[:H]
            dense_b[tx, ty, :, c * B : (c + 1) * B] = tile[H:]
        return carry

    lax.fori_loop(0, nt // 2, place, 0)
    for made in dy:
        made.wait_recv()
    total = buf["dy_send"][y] + 1.0
    for d in range(1, ny):
        total = total + buf["dy_recv"][d]
    root = lax.rsqrt(total)
    buf["roots"][me_t] = root
    exchanged = [
        links.copy(
            buf["roots"].at[me_t], buf["roots"].at[me_t], {"tgt": lax.rem(me_t + d, ns)}
        )
        for d in range(1, ns)
    ]
    gather_step(gathered, 1)
    lax.fori_loop(nt // 2, nt, place, 0)
    for k in range(2, nz // 2):
        gather_step(gathered, k)
    own_root = jnp.broadcast_to(root[0:1], (B, B)).T
    scaled1[...] = (own_root * feat[...].astype(F32)).astype(BF16)
    gather_finish(gathered)
    for made in exchanged:
        made.wait_recv()
    roots_t = buf["roots"][...].reshape(ns * 8, B).T
    for c in range(ns):
        ready1[c] = (roots_t[:, 8 * c : 8 * c + 1] * buf["src1"][c].astype(F32)).astype(BF16)

    def spread(layer, width):
        source = ready1 if layer == 1 else buf["src2"]
        blocks = min(4, ns)

        def product(panel, acc, n2):
            def step(k, carry):
                left = panel[:, :, pl.ds(pl.multiple_of(k * blocks * B, B), blocks * B)]
                right = source[pl.ds(k * blocks, blocks)].reshape(blocks * B, width)
                got = jnp.dot(left.reshape(n2 * H, blocks * B), right, preferred_element_type=F32)
                got = got.reshape(n2, H, width)

                @pl.when(k == 0)
                def _():
                    acc[:, :, 0:width] = got

                @pl.when(k > 0)
                def _():
                    acc[:, :, 0:width] += got

                return carry

            lax.fori_loop(0, ns // blocks, step, 0)

        class Chain:
            def __init__(self, name, dense, accs, n1, n2, p1, p2, at1, at2):
                self.name, self.dense, self.accs = name, dense, accs
                self.n1, self.n2, self.p1, self.p2, self.at1, self.at2 = n1, n2, p1, p2, at1, at2
                self.steps1 = (n1 // 2, (n1 - 1) // 2)
                self.steps2 = (n2 // 2, (n2 - 1) // 2)
                self.made1, self.made2 = ({}, {}), ({}, {})
                self.size = 2 if n2 % 2 == 0 else 1
                self.subs = n2 // self.size

            def refs(self, phase, way):
                key = f"{self.name}{phase}{way}{layer}"
                return buf[key + "send"], buf[key + "recv"]

            def multiply(self, way, k):
                d = sign if way == 0 else -sign
                place = wrap(self.p1 + d * (self.steps1[way] - k), self.n1)
                product(self.dense.at[place], self.accs[way], self.n2)

            def multiply_own(self):
                product(self.dense.at[self.p1], self.accs[2], self.n2)

            def send1(self, way, k, j):
                d = sign if way == 0 else -sign
                send, recv = self.refs(1, way)
                at = pl.ds(j * self.size, self.size)
                value = self.accs[way][at, :, 0:width]
                if k:
                    self.made1[way][k - 1, j].wait_recv()
                    value = value + recv[k - 1, at].astype(F32)
                send[k, at] = value.astype(BF16)
                self.made1[way][k, j] = links.copy(send.at[k, at], recv.at[k, at], self.at1(d))

            def middle(self, j):
                at = pl.ds(j * self.size, self.size)
                value = self.accs[2][at, :, 0:width]
                for way, steps in enumerate(self.steps1):
                    if steps:
                        self.made1[way][steps - 1, j].wait_recv()
                        value = value + self.refs(1, way)[1][steps - 1, at].astype(F32)
                self.accs[2][at, :, 0:width] = value

            def send2(self, way, k):
                d = sign if way == 0 else -sign
                send, recv = self.refs(2, way)
                value = self.accs[2][wrap(self.p2 + d * (self.steps2[way] - k), self.n2), :, 0:width]
                if k:
                    self.made2[way][k - 1].wait_recv()
                    value = value + recv[k - 1].astype(F32)
                send[k] = value.astype(BF16)
                self.made2[way][k] = links.copy(send.at[k], recv.at[k], self.at2(d))

            def end(self):
                value = self.accs[2][self.p2, :, 0:width]
                for way, steps in enumerate(self.steps2):
                    if steps:
                        self.made2[way][steps - 1].wait_recv()
                        value = value + self.refs(2, way)[1][steps - 1].astype(F32)
                return value

            def events(self, unit, shift):
                found = []
                for way, steps in enumerate(self.steps1):
                    for k in range(steps):
                        before = (k - 1) * unit + 0.5 * unit / self.subs if k else -1.0
                        found.append((before + shift + 0.1 * way, functools.partial(self.multiply, way, k)))
                        for j in range(self.subs):
                            at = (k - 1) * unit + unit * (j + 1) / self.subs if k else -1.0
                            found.append((at + shift + 0.1 * way, functools.partial(self.send1, way, k, j)))
                last = max(self.steps1) * unit
                found.append((last - unit + 0.5 * unit / self.subs + shift, self.multiply_own))
                for j in range(self.subs):
                    found.append((last - unit + unit * (j + 1) / self.subs + shift, functools.partial(self.middle, j)))
                for way, steps in enumerate(self.steps2):
                    for k in range(steps):
                        at = last + 0.01 + 0.8 * k
                        found.append((at + shift + 0.1 * way, functools.partial(self.send2, way, k)))
                return found

        a = Chain("a", dense_a, accs_a, ny, nx, y, x, at_y, at_x)
        b = Chain("b", dense_b, accs_b, nx, ny, x, y, at_x, at_y)
        events = a.events(1.0, 0.0) + b.events(a.steps1[0] / max(b.steps1[0], 1), 0.05)
        for _, event in sorted(events, key=lambda entry: entry[0]):
            event()
        return a.end, b.end

    def finish_rows(end, first, scaled, weight):
        summed = end()
        root_b = jnp.concatenate([own_root[first : first + H]] * (summed.shape[1] // B), axis=1)
        combined = (root_b * (summed + scaled.astype(F32))).astype(BF16)
        got = jnp.dot(combined, weight[...], preferred_element_type=F32)
        return jnp.maximum(got, 0.0).astype(BF16)

    width1, width2 = feat.shape[1], w1.shape[1]
    gathers = []
    for half, end in enumerate(spread(1, width1)):
        rows = slice(half * H, (half + 1) * H)
        hidden = finish_rows(end, half * H, scaled1[rows], w1)
        root_2 = jnp.concatenate([own_root[rows]] * (width2 // B), axis=1)
        buf["src2"][me_t, rows] = (root_2 * hidden.astype(F32)).astype(BF16)
        gathers.append(gather_start(buf["src2"], half * H, H))
    for k in range(nz // 2):
        for state in gathers:
            gather_step(state, k)
    for state in gathers:
        gather_finish(state)
    for half, end in enumerate(spread(2, width2)):
        rows = slice(half * H, (half + 1) * H)
        out[rows] = finish_rows(end, half * H, buf["src2"][me_t, rows], w2)
    links.finish()


def on_device(dims, features, adjacency, tile_slot, tile_live, first_weight, second_weight):
    nx, ny, nz = dims
    nt, ns = nx * ny, 2 * nz
    count = adjacency.shape[2]
    width1, width2 = first_weight.shape
    rows = plan(nx, ny, nz, width1, width2)
    copies = 300
    vmem = pl.BlockSpec(memory_space=pltpu.VMEM)
    group = min(16, count // LOADS)
    return pl.pallas_call(
        functools.partial(kernel, dims, [name for name, _, _ in rows]),
        out_shape=jax.ShapeDtypeStruct((B, second_weight.shape[1]), BF16),
        in_specs=[vmem, pl.BlockSpec(memory_space=pl.ANY), vmem, vmem, vmem, vmem],
        out_specs=vmem,
        scratch_shapes=[pltpu.VMEM(shape, dtype) for _, shape, dtype in rows]
        + [
            pltpu.VMEM((count, B, B), BF16),
            pltpu.VMEM((count + 1, B, B), BF16),
            pltpu.VMEM((count // group, group, B), F32),
            pltpu.VMEM((ny, nx, H, ns * B), BF16),
            pltpu.VMEM((nx, ny, H, ns * B), BF16),
            *[pltpu.VMEM((nx, H, width2), F32)] * 3,
            *[pltpu.VMEM((ny, H, width2), F32)] * 3,
            pltpu.VMEM((ns, B, width1), BF16),
            pltpu.VMEM((B, width1), BF16),
            pltpu.VMEM((8, B), jnp.int32),
            pltpu.SMEM((8, B), jnp.int32),
            pltpu.SemaphoreType.DMA((LOADS,)),
            pltpu.SemaphoreType.DMA,
            pltpu.SemaphoreType.DMA((copies,)),
            pltpu.SemaphoreType.DMA((copies,)),
        ],
        compiler_params=pltpu.CompilerParams(
            collective_id=0, has_side_effects=True, vmem_limit_bytes=56 * 2**20
        ),
    )(
        features,
        adjacency[0, 0],
        tile_slot[0],
        tile_live[0],
        first_weight,
        second_weight,
    )


def solution(mesh, nx=NX):
    dims = (nx, mesh.shape["src"] // nx, mesh.shape["tgt"] // 2)
    placed = (
        P(("tgt", "src"), None),
        P("tgt", "src", None, None, None),
        P("tgt", "src", None),
        P("tgt", "src", None),
        P(),
        P(),
    )
    return jax.shard_map(
        functools.partial(on_device, dims),
        mesh=mesh,
        in_specs=placed,
        out_specs=P(("tgt", "src"), None),
        check_vma=False,
    )
```

time: 808 us -> 117 us (0.14)
  the two profiles are of different devices: /device:TPU:16 before, /device:TPU:2 now
where the time goes in v1:
time: 117 us
  Pallas kernels  115 us (98%)
  local copies, waits for them, and re-layouts  1.47 us (1%)
    pallas_call x1, Pallas kernels, on_device(): pl.pallas_call(functools.partial(kernel, dims, [name for name, _, _ in ro...  115 us

profile of v1, /device:TPU:2, one launch (start us, length us, event | category | flops | bytes accessed | tf_op | source)
XLA Modules:
  0.0 116.6 jit_solution(15458541431137859362)
XLA Ops:
  0.0 115.1 %shard_map.64 = bf16[128,256]{1,0:T(8,128)(2,1)} custom-call(bf16[128,128]{1,0:T(8,128)(2,1)} %feat.1, bf16[128,128,128]{2,1,0:T(8,128)(2,1)} %bitcast.3, s32[1,128]{1,0:T(1,128)} %bitcast.4, s32[1,128]{1,0:T(1,128)} %bitcast.5, bf16[128,256]{1,0:T(8,128)(2,1)} %w1.1, bf16[256,256]{1,0:T(8,128)(2,1)} %w2.1), custom_call_target="tpu_custom_call" | custom-call | tf_op jit(solution)/shard_map/pallas_call | solution.py:412
  115.1 1.5 %copy.8 = bf16[128,256]{1,0:T(8,128)(2,1)} copy(bf16[128,256]{1,0:T(8,128)(2,1)} %shard_map.64) | data formatting | bytes 131072

commit v2 on v1

--- a/solution.py
+++ b/solution.py
@@ -48,7 +48,7 @@
         self.count = 0
         self.sent = []
 
-    def copy(self, src, dst, device):
+    def make(self, src, dst, device):
         number = self.count
         self.count += 1
         made = pltpu.make_async_remote_copy(
@@ -59,8 +59,12 @@
             device_id=device,
             device_id_type=MESH,
         )
+        self.sent.append(made)
+        return made
+
+    def copy(self, src, dst, device):
+        made = self.make(src, dst, device)
         made.start()
-        self.sent.append(made)
         return made
 
     def finish(self):
@@ -96,9 +100,7 @@
     nb = nt * ns
     count = adj.shape[0]
     buf = dict(zip(names, scratch))
-    (tiles, sums, rowsum, dense_a, dense_b, acc_a0, acc_a1, acc_a2, acc_b0, acc_b1, acc_b2,
-     ready1, scaled1, index_v, index_s, load_sems, index_sem, send_sems, recv_sems) = scratch[len(names):]
-    accs_a, accs_b = (acc_a0, acc_a1, acc_a2), (acc_b0, acc_b1, acc_b2)
+    (tiles, sums, rowsum, dense, acc, ready1, scaled1, index_v, index_s, load_sems, index_sem, send_sems, recv_sems) = scratch[len(names):]
     links = Links(send_sems, recv_sems)
 
     me_s, me_t = lax.axis_index("src"), lax.axis_index("tgt")
@@ -229,13 +231,21 @@
     ]
     gather_step(gathered, 0)
 
-    def place(t, carry):
-        ty, tx = t // nx, lax.rem(t, nx)
+    halves = ny // nx
+
+    def distance(i, n):
+        h, short = i // 2, lax.rem(i, 2)
+        return sign * ((n // 2 - h) * (1 - short) - ((n - 1) // 2 - h) * short)
+
+    def place(u, carry):
+        i, r = u // nx, lax.rem(u, nx)
+        t_a = wrap(y + distance(i, ny), ny) * nx + r
+        t_b = (lax.rem(i, halves) * nx + r) * nx + wrap(x + distance(i // halves, nx), nx)
         for c in range(ns):
-            v = t * ns + c
-            tile = sums[jnp.clip(index_s[2 + v // B, lax.rem(v, B)], 0, count)]
-            dense_a[ty, tx, :, c * B : (c + 1) * B] = tile[:H]
-            dense_b[tx, ty, :, c * B : (c + 1) * B] = tile[H:]
+            for part, t in enumerate((t_a, t_b)):
+                v = t * ns + c
+                found = jnp.clip(index_s[2 + v // B, lax.rem(v, B)], 0, count)
+                dense[i, part, r, :, c * B : (c + 1) * B] = sums[found, part * H : (part + 1) * H]
         return carry
 
     lax.fori_loop(0, nt // 2, place, 0)
@@ -267,30 +277,9 @@
 
     def spread(layer, width):
         source = ready1 if layer == 1 else buf["src2"]
-        blocks = min(4, ns)
-
-        def product(panel, acc, n2):
-            def step(k, carry):
-                left = panel[:, :, pl.ds(pl.multiple_of(k * blocks * B, B), blocks * B)]
-                right = source[pl.ds(k * blocks, blocks)].reshape(blocks * B, width)
-                got = jnp.dot(left.reshape(n2 * H, blocks * B), right, preferred_element_type=F32)
-                got = got.reshape(n2, H, width)
-
-                @pl.when(k == 0)
-                def _():
-                    acc[:, :, 0:width] = got
-
-                @pl.when(k > 0)
-                def _():
-                    acc[:, :, 0:width] += got
-
-                return carry
-
-            lax.fori_loop(0, ns // blocks, step, 0)
-
         class Chain:
-            def __init__(self, name, dense, accs, n1, n2, p1, p2, at1, at2):
-                self.name, self.dense, self.accs = name, dense, accs
+            def __init__(self, name, part, n1, n2, p1, p2, at1, at2):
+                self.name, self.part = name, part
                 self.n1, self.n2, self.p1, self.p2, self.at1, self.at2 = n1, n2, p1, p2, at1, at2
                 self.steps1 = (n1 // 2, (n1 - 1) // 2)
                 self.steps2 = (n2 // 2, (n2 - 1) // 2)
@@ -302,38 +291,55 @@
                 key = f"{self.name}{phase}{way}{layer}"
                 return buf[key + "send"], buf[key + "recv"]
 
-            def multiply(self, way, k):
-                d = sign if way == 0 else -sign
-                place = wrap(self.p1 + d * (self.steps1[way] - k), self.n1)
-                product(self.dense.at[place], self.accs[way], self.n2)
-
-            def multiply_own(self):
-                product(self.dense.at[self.p1], self.accs[2], self.n2)
+            def term(self, place, first, size):
+                if self.part == 0:
+                    return acc.at[place, 0, pl.ds(first, size), :, 0:width]
+                lead = place * halves + first // nx
+                return acc.at[lead, 1, pl.ds(lax.rem(first, nx), size), :, 0:width]
+
+            def first(self, way):
+                if not self.steps1[way]:
+                    return
+                send, recv = self.refs(1, way)
+                for j in range(self.subs):
+                    at = pl.ds(j * self.size, self.size)
+                    self.made1[way][0, j] = links.make(
+                        send.at[0, at], recv.at[0, at], self.at1(sign if way == 0 else -sign)
+                    )
+
+            def start_first(self, way):
+                if not self.steps1[way]:
+                    return
+                send = self.refs(1, way)[0]
+                for j in range(self.subs):
+                    at = pl.ds(j * self.size, self.size)
+                    send[0, at] = self.term(way, j * self.size, self.size)[...].astype(BF16)
+                    self.made1[way][0, j].start()
 
             def send1(self, way, k, j):
                 d = sign if way == 0 else -sign
                 send, recv = self.refs(1, way)
                 at = pl.ds(j * self.size, self.size)
-                value = self.accs[way][at, :, 0:width]
-                if k:
-                    self.made1[way][k - 1, j].wait_recv()
-                    value = value + recv[k - 1, at].astype(F32)
-                send[k, at] = value.astype(BF16)
+                value = self.term(2 * k + way, j * self.size, self.size)[...]
+                self.made1[way][k - 1, j].wait_recv()
+                send[k, at] = (value + recv[k - 1, at].astype(F32)).astype(BF16)
                 self.made1[way][k, j] = links.copy(send.at[k, at], recv.at[k, at], self.at1(d))
 
             def middle(self, j):
                 at = pl.ds(j * self.size, self.size)
-                value = self.accs[2][at, :, 0:width]
+                term = self.term(self.n1 - 1, j * self.size, self.size)
+                value = term[...]
                 for way, steps in enumerate(self.steps1):
                     if steps:
                         self.made1[way][steps - 1, j].wait_recv()
                         value = value + self.refs(1, way)[1][steps - 1, at].astype(F32)
-                self.accs[2][at, :, 0:width] = value
+                term[...] = value
 
             def send2(self, way, k):
                 d = sign if way == 0 else -sign
                 send, recv = self.refs(2, way)
-                value = self.accs[2][wrap(self.p2 + d * (self.steps2[way] - k), self.n2), :, 0:width]
+                place = wrap(self.p2 + d * (self.steps2[way] - k), self.n2)
+                value = self.term(self.n1 - 1, place, 1)[...][0]
                 if k:
                     self.made2[way][k - 1].wait_recv()
                     value = value + recv[k - 1].astype(F32)
@@ -341,7 +347,7 @@
                 self.made2[way][k] = links.copy(send.at[k], recv.at[k], self.at2(d))
 
             def end(self):
-                value = self.accs[2][self.p2, :, 0:width]
+                value = self.term(self.n1 - 1, self.p2, 1)[...][0]
                 for way, steps in enumerate(self.steps2):
                     if steps:
                         self.made2[way][steps - 1].wait_recv()
@@ -351,14 +357,11 @@
             def events(self, unit, shift):
                 found = []
                 for way, steps in enumerate(self.steps1):
-                    for k in range(steps):
-                        before = (k - 1) * unit + 0.5 * unit / self.subs if k else -1.0
-                        found.append((before + shift + 0.1 * way, functools.partial(self.multiply, way, k)))
+                    for k in range(1, steps):
                         for j in range(self.subs):
-                            at = (k - 1) * unit + unit * (j + 1) / self.subs if k else -1.0
+                            at = (k - 1) * unit + unit * (j + 1) / self.subs
                             found.append((at + shift + 0.1 * way, functools.partial(self.send1, way, k, j)))
                 last = max(self.steps1) * unit
-                found.append((last - unit + 0.5 * unit / self.subs + shift, self.multiply_own))
                 for j in range(self.subs):
                     found.append((last - unit + unit * (j + 1) / self.subs + shift, functools.partial(self.middle, j)))
                 for way, steps in enumerate(self.steps2):
@@ -367,8 +370,24 @@
                         found.append((at + shift + 0.1 * way, functools.partial(self.send2, way, k)))
                 return found
 
-        a = Chain("a", dense_a, accs_a, ny, nx, y, x, at_y, at_x)
-        b = Chain("b", dense_b, accs_b, nx, ny, x, y, at_x, at_y)
+        a = Chain("a", 0, ny, nx, y, x, at_y, at_x)
+        b = Chain("b", 1, nx, ny, x, y, at_x, at_y)
+        for way in range(2):
+            a.first(way)
+            b.first(way)
+
+        def multiply(i, carry):
+            right = source[...].reshape(ns * B, width)
+            for part in range(2):
+                left = dense[i, part].reshape(nx * H, ns * B)
+                got = jnp.dot(left, right, preferred_element_type=F32)
+                acc[i, part, :, :, 0:width] = got.reshape(nx, H, width)
+            for way in range(2):
+                pl.when(i == way)(functools.partial(a.start_first, way))
+                pl.when(i == (way + 1) * halves - 1)(functools.partial(b.start_first, way))
+            return carry
+
+        lax.fori_loop(0, ny, multiply, 0)
         events = a.events(1.0, 0.0) + b.events(a.steps1[0] / max(b.steps1[0], 1), 0.05)
         for _, event in sorted(events, key=lambda entry: entry[0]):
             event()
@@ -419,10 +438,8 @@
             pltpu.VMEM((count, B, B), BF16),
             pltpu.VMEM((count + 1, B, B), BF16),
             pltpu.VMEM((count // group, group, B), F32),
-            pltpu.VMEM((ny, nx, H, ns * B), BF16),
-            pltpu.VMEM((nx, ny, H, ns * B), BF16),
-            *[pltpu.VMEM((nx, H, width2), F32)] * 3,
-            *[pltpu.VMEM((ny, H, width2), F32)] * 3,
+            pltpu.VMEM((ny, 2, nx, H, ns * B), BF16),
+            pltpu.VMEM((ny, 2, nx, H, width2), F32),
             pltpu.VMEM((ns, B, width1), BF16),
             pltpu.VMEM((B, width1), BF16),
             pltpu.VMEM((8, B), jnp.int32),

time: 117 us -> 116 us (level)
  no operation moved by 1% of the time
where the time goes in v2:
time: 116 us
  Pallas kernels  114 us (98%)
  local copies, waits for them, and re-layouts  1.47 us (1%)
    pallas_call x1, Pallas kernels, on_device(): pl.pallas_call(functools.partial(kernel, dims, [name for name, _, _ in ro...  114 us

profile of v2, /device:TPU:2, one launch (start us, length us, event | category | flops | bytes accessed | tf_op | source)
XLA Modules:
  0.0 115.6 jit_solution(17620208663730419465)
XLA Ops:
  0.0 114.1 %shard_map.64 = bf16[128,256]{1,0:T(8,128)(2,1)} custom-call(bf16[128,128]{1,0:T(8,128)(2,1)} %feat.1, bf16[128,128,128]{2,1,0:T(8,128)(2,1)} %bitcast.3, s32[1,128]{1,0:T(1,128)} %bitcast.4, s32[1,128]{1,0:T(1,128)} %bitcast.5, bf16[128,256]{1,0:T(8,128)(2,1)} %w1.1, bf16[256,256]{1,0:T(8,128)(2,1)} %w2.1), custom_call_target="tpu_custom_call" | custom-call | tf_op jit(solution)/shard_map/pallas_call | solution.py:431
  114.1 1.5 %copy.8 = bf16[128,256]{1,0:T(8,128)(2,1)} copy(bf16[128,256]{1,0:T(8,128)(2,1)} %shard_map.64) | data formatting | bytes 131072

commit v3 on v2

--- a/solution.py
+++ b/solution.py
@@ -284,7 +284,7 @@
                 self.steps1 = (n1 // 2, (n1 - 1) // 2)
                 self.steps2 = (n2 // 2, (n2 - 1) // 2)
                 self.made1, self.made2 = ({}, {}), ({}, {})
-                self.size = 2 if n2 % 2 == 0 else 1
+                self.size = 4 if n2 % 4 == 0 else 1
                 self.subs = n2 // self.size
 
             def refs(self, phase, way):

time: 116 us -> 118 us (1.017)
  Pallas kernels: 114 us -> 116 us
    pallas_call x1, Pallas kernels: 114 us -> 116 us  [on_device(): pl.pallas_call(functools.partial(kernel, dims, [name for name, _, _ in ro...]
where the time goes in v3:
time: 118 us
  Pallas kernels  116 us (98%)
  local copies, waits for them, and re-layouts  1.47 us (1%)
    pallas_call x1, Pallas kernels, on_device(): pl.pallas_call(functools.partial(kernel, dims, [name for name, _, _ in ro...  116 us

profile of v3, /device:TPU:2, one launch (start us, length us, event | category | flops | bytes accessed | tf_op | source)
XLA Modules:
  0.0 117.8 jit_solution(11653140970714170001)
XLA Ops:
  0.0 116.3 %shard_map.64 = bf16[128,256]{1,0:T(8,128)(2,1)} custom-call(bf16[128,128]{1,0:T(8,128)(2,1)} %feat.1, bf16[128,128,128]{2,1,0:T(8,128)(2,1)} %bitcast.3, s32[1,128]{1,0:T(1,128)} %bitcast.4, s32[1,128]{1,0:T(1,128)} %bitcast.5, bf16[128,256]{1,0:T(8,128)(2,1)} %w1.1, bf16[256,256]{1,0:T(8,128)(2,1)} %w2.1), custom_call_target="tpu_custom_call" | custom-call | tf_op jit(solution)/shard_map/pallas_call | solution.py:431
  116.3 1.5 %copy.8 = bf16[128,256]{1,0:T(8,128)(2,1)} copy(bf16[128,256]{1,0:T(8,128)(2,1)} %shard_map.64) | data formatting | bytes 131072
